TPU v7x, 32 devices: a whole 2x2x4 slice. The times are simulated.
32 devices in a mesh: segment: 2 (over core), seq: 16 (over z, y, x).
Axes of the slice: x: 2, y: 2, z: 4, core: 2. Of those that a mesh axis runs over, the one named last changes fastest.
Arguments:
- hidden: bfloat16 [2048, 2560], P('seq'), may hold values from -6 to 6
- norm_gain: float32 [2, 2560], P('segment'), may hold values from 0.1 to 1.9
- query_weight: bfloat16 [2, 2560, 2560], P('segment'), as said below
- key_weight: bfloat16 [2, 2560, 512], P('segment'), as said below
- value_weight: bfloat16 [2, 2560, 512], P('segment'), may hold values from -0.125 to 0.125
- owned_block: int32 [16], replicated, may hold values from 0 to 15, as said below
Outputs:
- layer_outputs: bfloat16 [2, 2048, 2560], P('segment', 'seq')
Inputs may be any that keep to these rules, and one draw needn't show every extreme that they name: `owned_block`: each aligned run of 16 devices holds the 16 blocks of one group, each once. `query_weight`: entries scaled by the fan-in. `key_weight`: entries scaled by the fan-in.
All inputs are finite; a program needn't handle non-finite values.
Results may differ from a plain program's by a relative error of at most 0.011.
Values may be sent and summed in bfloat16 or wider, within the bound.
A program may use at most 192 MiB of HBM per device.

v0:
```python
import jax
import jax.numpy as jnp
from jax import lax
from jax.sharding import PartitionSpec as P

HS = 128
PB = 8
NC = 4
CB = 2
GROUP = 16


rope_base = 1000000.0
neg_fill = -1e30
norm_eps = 1e-06


def shifted(value, axis, steps):
    count = lax.axis_size(axis)
    leading, last = (max(0, -steps), min(count, count - steps))
    return lax.ppermute(value, axis, [(source, source + steps) for source in range(leading, last)])


def block_meta(block_ids, row_ids, block_rows):
    local_id = block_ids % GROUP
    is_prompt = local_id < PB
    sequence = jnp.where(is_prompt, NC, (local_id - PB) // CB)
    place = jnp.where(is_prompt, local_id, PB + (local_id - PB) % CB)
    return (block_ids // GROUP, is_prompt, sequence, place * block_rows + row_ids)


def rotate(values, positions):
    half_dim = values.shape[-1] // 2
    freqs = rope_base ** (-(jnp.arange(half_dim, dtype=jnp.float32) * 2.0 / values.shape[-1]))
    angles = positions.astype(jnp.float32)[:, None] * freqs[None, :]
    cosine = jnp.cos(angles)[:, None, :]
    sine = jnp.sin(angles)[:, None, :]
    front = values[..., :half_dim]
    back = values[..., half_dim:]
    return jnp.concatenate([front * cosine - back * sine, back * cosine + front * sine], axis=-1)


def project(hidden_rows, gain, w_query, w_key, w_value, positions):
    count = hidden_rows.shape[0]
    widened = hidden_rows.astype(jnp.float32)
    meansq = jnp.mean(widened * widened, axis=-1, keepdims=True)
    normed = (widened * lax.rsqrt(meansq + norm_eps) * gain).astype(jnp.bfloat16)
    query = jnp.dot(normed, w_query, preferred_element_type=jnp.float32).reshape(count, -1, HS)
    query = (rotate(query, positions) * HS ** (-0.5)).astype(jnp.bfloat16)
    key_part = jnp.dot(normed, w_key, preferred_element_type=jnp.float32).reshape(count, -1, HS)
    key_part = rotate(key_part, positions).astype(jnp.bfloat16).reshape(count, -1)
    value_part = jnp.dot(normed, w_value, preferred_element_type=jnp.float32).astype(jnp.bfloat16)
    return (query, key_part, value_part)


def attend(state_now, query, query_info, key_rows, value_rows, key_info):
    top_now, total_now, accum = state_now
    q_grp, q_prompt, q_seq, q_pos = query_info
    k_grp, k_prompt, k_seq, k_pos = key_info
    allowed = (k_grp[None, :] == q_grp[:, None]) & (
        k_prompt[None, :] & jnp.logical_not(q_prompt[:, None])
        | (k_seq[None, :] == q_seq[:, None]) & (k_pos[None, :] <= q_pos[:, None])
    )
    count = key_rows.shape[0]
    kv_heads = query.shape[0]
    keys_split = key_rows.reshape(count, kv_heads, -1)
    values_split = value_rows.reshape(count, kv_heads, -1)
    scores = jnp.einsum("grnd,lgd->grnl", query, keys_split, preferred_element_type=jnp.float32)
    scores = jnp.where(allowed[None, None], scores, neg_fill)
    top_new = jnp.maximum(top_now, jnp.max(scores, axis=-1))
    weights = jnp.where(allowed[None, None], jnp.exp(scores - top_new[..., None]), 0.0)
    rescale = jnp.exp(top_now - top_new)
    total_new = total_now * rescale + jnp.sum(weights, axis=-1)
    update = jnp.einsum(
        "grnl,lgd->grnd",
        weights.astype(jnp.bfloat16),
        values_split,
        preferred_element_type=jnp.float32,
    )
    return (top_new, total_new, accum * rescale[..., None] + update)


def local(hidden, norm_gain, query_weight, key_weight, value_weight, owned_block):
    rows_dev = hidden.shape[0]
    head_count = query_weight.shape[2] // HS
    kv_count = key_weight.shape[2] // HS
    repeat_count = head_count // kv_count
    seq_index = lax.axis_index("seq")
    segment_index = lax.axis_index("segment")
    gain = norm_gain[0]
    w_query = query_weight[0]
    w_key = key_weight[0]
    w_value = value_weight[0]
    row_ids = jnp.arange(rows_dev, dtype=jnp.int32)
    my_block = jnp.full((rows_dev,), owned_block[seq_index], jnp.int32)
    query_info = block_meta(my_block, row_ids, rows_dev)
    my_group = owned_block[seq_index] // GROUP

    def remote_info(device_rows, row_in_block):
        grp, prompt, sequence, place = block_meta(owned_block[device_rows], row_in_block, rows_dev)
        grp = jnp.where(device_rows == seq_index, -1, grp)
        return (grp, prompt, sequence, place)

    def fold_part(state_in, key_rows, value_rows, first_row):
        ids = first_row + jnp.arange(key_rows.shape[0], dtype=jnp.int32)
        info = remote_info(ids // rows_dev, ids % rows_dev)
        needed = jnp.any(info[0] == my_group)

        def take(state_take):
            return attend(state_take, query_now[0], query_info, key_rows, value_rows, info)

        def leave(state_leave):
            return state_leave

        return lax.cond(needed, take, leave, state_in)

    query_now = [None]

    def fold_piece(state_now, pieces, start):
        key_rows, value_rows = pieces
        count = key_rows.shape[0]
        span = GROUP * rows_dev
        if count > span and count % span == 0:
            key_blocks = key_rows.reshape(count // span, span, -1)
            value_blocks = value_rows.reshape(count // span, span, -1)
            starts = start + span * jnp.arange(count // span, dtype=jnp.int32)

            def step(state_in, item):
                return (fold_part(state_in, item[0], item[1], item[2]), None)

            state_now, _ = lax.scan(step, state_now, (key_blocks, value_blocks, starts))
            return state_now
        return fold_part(state_now, key_rows, value_rows, start)

    def layer_call(layer_input):
        query, key_rows, value_rows = project(
            layer_input, gain, w_query, w_key, w_value, query_info[3]
        )
        query = query.reshape(rows_dev, kv_count, repeat_count, HS).transpose(1, 2, 0, 3)
        query_now[0] = query
        state_now = (
            jnp.full((kv_count, repeat_count, rows_dev), neg_fill, jnp.float32),
            jnp.zeros((kv_count, repeat_count, rows_dev), jnp.float32),
            jnp.zeros((kv_count, repeat_count, rows_dev, HS), jnp.float32),
        )
        state_now = attend(state_now, query, query_info, key_rows, value_rows, query_info)
        state_now = fold_piece(
            state_now,
            (
                lax.all_gather(key_rows, "seq", axis=0, tiled=True),
                lax.all_gather(value_rows, "seq", axis=0, tiled=True),
            ),
            jnp.int32(0),
        )
        top_now, total_now, accum = state_now
        mixed = accum / total_now[..., None]
        heads_out = mixed.transpose(2, 0, 1, 3).reshape(rows_dev, head_count * HS)
        return (layer_input.astype(jnp.float32) + heads_out).astype(jnp.bfloat16)

    first_out = layer_call(hidden)
    handed = shifted(first_out, "segment", 1)
    second_out = layer_call(handed)
    result = jnp.where(segment_index == 0, first_out, second_out)
    return result[None]


def solution(mesh):
    return jax.shard_map(
        local,
        mesh=mesh,
        in_specs=(
            P("seq", None),
            P("segment", None),
            P("segment", None, None),
            P("segment", None, None),
            P("segment", None, None),
            P(),
        ),
        out_specs=P("segment", "seq", None),
        check_vma=False,
    )
```

profile of v0, /device:TPU:1, one launch (start us, length us, event | category | flops | bytes accessed | tf_op | source)
XLA Modules:
  0.0 358.2 jit_solution(3416587153460467283)
XLA Ops:
  12.5 4.4 %copy.94 = bf16[512,2560]{1,0:T(8,128)(2,1)} copy(bf16[512,2560]{0,1:T(8,128)(2,1)} %bitcast.101) | data formatting | bytes 5242880 | tf_op jit(solution)/shard_map/dot_general | solution.py:50
  17.2 2.7 fusion.63
  26.9 4.4 %compare_select_fusion.1 = s32[2048,1]{0,1:T(1,128)S(1)} fusion(s32[]{:T(128)} %bitcast.13, s32[]{:T(128)} %bitcast.14, s32[]{:T(128)} %bitcast.15, s32[]{:T(128)} %bitcast.16, s32[]{:T(128)} %bitcast.17, s32[]{:T(128)} %bitcast.19, s32[]{:T(128)} %bitcast.18), kind=kLoop, calls=%fused_computation.110 | loop fusion | flops 47104 | bytes 8220 | tf_op jit(solution)/shard_map/gather | solution.py:100
  31.3 6.3 %fusion.89 = (s32[2048]{0:T(1024)}, s32[2048]{0:T(1024)S(1)}) fusion(pred[2048]{0:T(1024)(128)(4,1)S(1)} %compare_reduce_fusion, pred[2048]{0:T(1024)(128)(4,1)S(1)} %compare_reduce_fusion.1, pred[2048]{0:T(1024)(128)(4,1)S(1)} %compare_reduce_fusion.2, pred[2048]{0:T(1024)(128)(4,1)S(1)} %compare_reduce_fusion.3, ...), kind=kLoop, calls=%fused_computation.148 | loop fusion | flops 88064 | bytes 43044 | tf_op jit(solution)/shard_map/add | solution.py:29
  39.5 17.6 %copy.34 = bf16[1,2560,2560]{1,2,0:T(8,128)(2,1)} copy(bf16[1,2560,2560]{2,1,0:T(8,128)(2,1)} %param.12) | data formatting | bytes 26214400 | tf_op args[2]
  57.1 6.8 %fusion.65 = f32[128,20,128]{0,2,1:T(8,128)S(1)} fusion(bf16[20,128,2560]{2,1,0:T(8,128)(2,1)} %bitcast.97, bf16[128,2560]{0,1:T(8,128)(2,1)S(1)} %copy.33, f32[2560]{0:T(1024)S(1)} %reduce.9, f32[128]{0:T(128)S(1)} %add_rsqrt_fusion.1), kind=kOutput, calls=%fused_computation.73 | convolution fusion | flops 1679032320 | bytes 15084032 | tf_op jit(solution)/shard_map/dot_general | solution.py:48
  76.2 8.6 %all-gather.5.cloned.1.call-done = bf16[2048,512]{1,0:T(8,128)(2,1)} async-done(((bf16[128,512]{1,0:T(8,128)(2,1)}), bf16[2048,512]{1,0:T(8,128)(2,1)}) %all-gather.5.cloned.1.call-update) | async-done | bytes 2097168 | tf_op jit(solution)/shard_map/all_gather | solution.py:150
  84.8 62.2 %all-gather.7.cloned.1.call-done = bf16[2048,512]{1,0:T(8,128)(2,1)} async-done(((bf16[128,512]{1,0:T(8,128)(2,1)}), bf16[2048,512]{1,0:T(8,128)(2,1)}) %all-gather.7.cloned.1.call-update) | async-done | bytes 2097168 | tf_op jit(solution)/shard_map/all_gather | solution.py:151
  148.1 37.1 %conditional.2 = (f32[4,5,128]{2,1,0:T(8,128)S(1)}, f32[4,5,128,128]{2,3,1,0:T(8,128)}) conditional(s32[]{:T(128)} %convert_element_type.75, (f32[4,5,128]{2,1,0:T(8,128)S(1)}, f32[4,5,128,128]{3,2,1,0:T(8,128)}) %tuple.19, (s32[2048]{0:T(1024)}, s32[128]{0:T(128)}, pred[2048]{0:T(1024)(128)(4,1)}, pred[128]{0:T(512)(128)(4,1)S(1)}, s32[2048]{0:T(1024)}, ...), branch_computations={%region_4.5_spmd, %region_5.8_spmd} | conditional | flops 2739278848 | bytes 166748240 | solution.py:115
  150.0 4.0 %reshape.456 = bf16[2048,4,128]{2,1,0:T(4,128)(2,1)} reshape(bf16[2048,512]{1,0:T(8,128)(2,1)} %get-tuple-element.80) | data formatting | bytes 4194304 | tf_op jit(solution)/shard_map/cond/branch_1_fun/reshape | solution.py:66
  154.0 4.8 %select_reduce_fusion = (f32[4,5,128]{2,1,0:T(8,128)S(1)}, f32[4,5,128,2048]{3,2,1,0:T(8,128)S(1)}) fusion(pred[128,2048]{1,0:T(8,128)(4,1)S(1)} %or_and_fusion, bf16[4,5,128,128]{3,2,1,0:T(8,128)(2,1)} %get-tuple-element.79, bf16[2048,4,128,1]{2,1,0,3:T(4,128)(2,1)} %bitcast.99), kind=kOutput, calls=%fused_computation.1 | convolution fusion | flops 1352660480 | bytes 23996416 | tf_op jit(solution)/shard_map/cond/branch_1_fun/grnd,lgd->grnl/dot_general | solution.py:68
  158.9 5.7 %fusion.1 = f32[4,5,128]{2,1,0:T(8,128)S(1)} fusion(f32[4,5,128,2048]{3,2,1,0:T(8,128)S(1)} %get-tuple-element.120, f32[4,5,128]{2,1,0:T(8,128)S(1)} %max.4, pred[128,2048]{1,0:T(8,128)(4,1)S(1)} %or_and_fusion), kind=kLoop, calls=%fused_computation.3 | loop fusion | flops 20968960 | bytes 21254144 | tf_op jit(solution)/shard_map/cond/branch_1_fun/reduce_sum | solution.py:73
  167.0 4.0 %reshape.457 = bf16[2048,4,128]{2,1,0:T(4,128)(2,1)} reshape(bf16[2048,512]{1,0:T(8,128)(2,1)} %get-tuple-element.82) | data formatting | bytes 4194304 | tf_op jit(solution)/shard_map/cond/branch_1_fun/reshape | solution.py:67
  171.0 11.4 %fusion.8 = f32[4,5,128,128]{3,2,1,0:T(8,128)} fusion(bf16[2048,4,128,1]{2,1,0,3:T(4,128)(2,1)} %bitcast.109, f32[4,5,128,2048]{3,2,1,0:T(8,128)} %copy-done.2, f32[4,5,128]{2,1,0:T(8,128)} %copy-done.24, pred[128,2048]{1,0:T(8,128)(4,1)S(1)} %or_and_fusion, f32[4,5,128,128]{3,2,1,0:T(8,128)} %get-tuple-element.81, f32[4,5,128]{2,1,0:T(8,128)} %get-tuple-element.112), kind=kOutput, calls=%fused_computation.9 | convolution fusion | flops 1363804160 | bytes 25972736 | tf_op jit(solution)/shard_map/cond/branch_1_fun/grnl,lgd->grnd/dot_general | solution.py:74
  182.4 2.9 copy.91
  188.5 2.7 collective-permute-done
  198.7 6.8 %fusion.61 = f32[128,20,128]{0,2,1:T(8,128)S(1)} fusion(bf16[20,128,2560]{2,1,0:T(8,128)(2,1)} %bitcast.98, bf16[128,2560]{0,1:T(8,128)(2,1)S(1)} %collective-permute-done, f32[128]{0:T(128)S(1)} %add_rsqrt_fusion, f32[2560]{0:T(1024)S(1)} %copy-done.19), kind=kOutput, calls=%fused_computation.69 | convolution fusion | flops 1679032320 | bytes 15084032 | tf_op jit(solution)/shard_map/dot_general | solution.py:48
  212.1 41.5 %all-gather.9.cloned.1.call-done = bf16[2048,512]{1,0:T(8,128)(2,1)} async-done(((bf16[128,512]{1,0:T(8,128)(2,1)}), bf16[2048,512]{1,0:T(8,128)(2,1)}) %all-gather.9.cloned.1.call-update) | async-done | bytes 2097168 | tf_op jit(solution)/shard_map/all_gather | solution.py:150
  253.6 62.0 %all-gather.11.cloned.1.call-done = bf16[2048,512]{1,0:T(8,128)(2,1)} async-done(((bf16[128,512]{1,0:T(8,128)(2,1)}), bf16[2048,512]{1,0:T(8,128)(2,1)}) %all-gather.11.cloned.1.call-update) | async-done | bytes 2097168 | tf_op jit(solution)/shard_map/all_gather | solution.py:151
  315.6 31.7 %conditional.3 = (f32[4,5,128]{2,1,0:T(8,128)S(1)}, f32[4,5,128,128]{2,3,1,0:T(8,128)S(1)}) conditional(s32[]{:T(128)} %convert_element_type.75, (f32[4,5,128]{2,1,0:T(8,128)S(1)}, f32[4,5,128,128]{3,2,1,0:T(8,128)}) %tuple.21, (s32[2048]{0:T(1024)S(1)}, s32[128]{0:T(128)S(1)}, pred[2048]{0:T(1024)(128)(4,1)S(1)}, pred[128]{0:T(512)(128)(4,1)S(1)}, ...), branch_computations={%region_11.12_spmd, %region_12.15_spmd} | conditional | flops 2739278848 | bytes 174366704 | solution.py:115
  319.3 4.1 %select_reduce_fusion.1 = (f32[4,5,128]{2,1,0:T(8,128)S(1)}, f32[4,5,128,2048]{3,2,1,0:T(8,128)S(1)}) fusion(pred[128,2048]{1,0:T(8,128)(4,1)S(1)} %or_and_fusion.1, bf16[4,5,128,128]{3,2,1,0:T(8,128)(2,1)} %copy-done.5, bf16[2048,4,128,1]{2,1,0,3:T(4,128)(2,1)S(1)} %bitcast.100), kind=kOutput, calls=%fused_computation.16 | convolution fusion | flops 1352660480 | bytes 23996416 | tf_op jit(solution)/shard_map/cond/branch_1_fun/grnd,lgd->grnl/dot_general | solution.py:68
  323.5 5.7 %fusion.16 = f32[4,5,128]{2,1,0:T(8,128)S(1)} fusion(f32[4,5,128,2048]{3,2,1,0:T(8,128)S(1)} %get-tuple-element.122, f32[4,5,128]{2,1,0:T(8,128)S(1)} %max.5, pred[128,2048]{1,0:T(8,128)(4,1)S(1)} %or_and_fusion.1), kind=kLoop, calls=%fused_computation.18 | loop fusion | flops 20968960 | bytes 21254144 | tf_op jit(solution)/shard_map/cond/branch_1_fun/reduce_sum | solution.py:73
  330.4 4.1 %reshape.459 = bf16[2048,4,128]{2,1,0:T(4,128)(2,1)} reshape(bf16[2048,512]{1,0:T(8,128)(2,1)} %get-tuple-element.96) | data formatting | bytes 4194304 | tf_op jit(solution)/shard_map/cond/branch_1_fun/reshape | solution.py:67
  334.5 11.1 %fusion.23 = f32[4,5,128,128]{3,2,1,0:T(8,128)} fusion(bf16[2048,4,128,1]{2,1,0,3:T(4,128)(2,1)} %bitcast.110, f32[4,5,128,2048]{3,2,1,0:T(8,128)} %copy-done.3, f32[4,5,128]{2,1,0:T(8,128)S(1)} %max.5, pred[128,2048]{1,0:T(8,128)(4,1)S(1)} %or_and_fusion.1, f32[4,5,128,128]{3,2,1,0:T(8,128)S(1)} %copy-done.6, f32[4,5,128]{2,1,0:T(8,128)S(1)} %get-tuple-element.114), kind=kOutput, calls=%fused_computation.24 | convolution fusion | flops 1363804160 | bytes 25972736 | tf_op jit(solution)/shard_map/cond/branch_1_fun/grnl,lgd->grnd/dot_general | solution.py:74
  (151 shorter events, 57.1 us)
Async XLA Ops:
  6.5 15.8 %copy-start = (bf16[1,2560,512]{2,1,0:T(8,128)(2,1)S(1)}, bf16[1,2560,512]{2,1,0:T(8,128)(2,1)}, u32[]{:S(2)}) copy-start(bf16[1,2560,512]{2,1,0:T(8,128)(2,1)} %param.14) | copy-start | bytes 7864324
  6.5 78.2 %all-gather.5.cloned.1.call-start = ((), (), s32[]{:S(2)}) async-start(), calls=%async_computation | async-start | bytes 2228224 | tf_op jit(solution)/shard_map/all_gather | solution.py:150
  16.9 40.2 %copy-start.18 = (f32[2560]{0:T(1024)}, f32[2560]{0:T(1024)S(1)}, u32[]{:S(2)}) copy-start(f32[2560]{0:T(1024)S(1)} %reduce.9) | copy-start | bytes 30724
  17.1 46.8 %copy-start.10 = (f32[128,64]{0,1:T(8,128)}, f32[128,64]{0,1:T(8,128)S(1)}, u32[]{:S(2)}) copy-start(f32[128,64]{0,1:T(8,128)S(1)} %get-tuple-element.136) | copy-start | bytes 98308
  17.1 46.8 %copy-start.12 = (f32[128,64]{0,1:T(8,128)}, f32[128,64]{0,1:T(8,128)S(1)}, u32[]{:S(2)}) copy-start(f32[128,64]{0,1:T(8,128)S(1)} %get-tuple-element.137) | copy-start | bytes 98308
  22.3 124.7 %all-gather.7.cloned.1.call-start = ((), (), s32[]{:S(2)}) async-start(), calls=%async_computation.1 | async-start | bytes 2228224 | tf_op jit(solution)/shard_map/all_gather | solution.py:151
  24.2 229.4 %all-gather.9.cloned.1.call-start = ((), (), s32[]{:S(2)}) async-start(), calls=%async_computation.2 | async-start | bytes 2228224 | tf_op jit(solution)/shard_map/all_gather | solution.py:150
  154.0 4.9 %copy-start.17 = (f32[4,5,128]{2,1,0:T(8,128)S(1)}, f32[4,5,128]{2,1,0:T(8,128)}, u32[]{:S(2)}) copy-start(f32[4,5,128]{2,1,0:T(8,128)} %get-tuple-element.70) | copy-start | bytes 30724 | tf_op jit(solution)/shard_map/cond
  158.9 7.0 %copy-start.2 = (f32[4,5,128,2048]{3,2,1,0:T(8,128)}, f32[4,5,128,2048]{3,2,1,0:T(8,128)S(1)}, u32[]{:S(2)}) copy-start(f32[4,5,128,2048]{3,2,1,0:T(8,128)S(1)} %get-tuple-element.120) | copy-start | bytes 62914564 | tf_op jit(solution)/shard_map/cond
  158.9 6.9 %copy-start.24 = (f32[4,5,128]{2,1,0:T(8,128)}, f32[4,5,128]{2,1,0:T(8,128)S(1)}, u32[]{:S(2)}) copy-start(f32[4,5,128]{2,1,0:T(8,128)S(1)} %max.4) | copy-start | bytes 30724 | tf_op jit(solution)/shard_map/cond
  158.9 6.9 %copy-start.21 = (f32[4,5,128]{2,1,0:T(8,128)S(1)}, f32[4,5,128]{2,1,0:T(8,128)}, u32[]{:S(2)}) copy-start(f32[4,5,128]{2,1,0:T(8,128)} %copy-done.20) | copy-start | bytes 30724 | tf_op jit(solution)/shard_map/cond
  186.7 4.8 %copy-start.7 = (bf16[512,2560]{1,0:T(8,128)(2,1)S(1)}, bf16[512,2560]{1,0:T(8,128)(2,1)}, u32[]{:S(2)}) copy-start(bf16[512,2560]{1,0:T(8,128)(2,1)} %copy.94) | copy-start | bytes 7864324
  186.7 4.8 %copy-start.19 = (f32[2560]{0:T(1024)S(1)}, f32[2560]{0:T(1024)}, u32[]{:S(2)}) copy-start(f32[2560]{0:T(1024)} %copy-done.18) | copy-start | bytes 30724
  186.9 4.3 %collective-permute-start = (bf16[128,2560]{0,1:T(8,128)(2,1)S(1)}, bf16[128,2560]{0,1:T(8,128)(2,1)S(1)}, u32[]{:S(2)}, u32[]{:S(2)}) collective-permute-start(bf16[128,2560]{0,1:T(8,128)(2,1)S(1)} %fusion.37), channel_id=1, source_target_pairs={{0,16},{1,17},{2,18},{3,19},{4,20},{5,21},{6,22},{7,23},{8,24},{9,... | collective-permute-start | bytes 1966088 | tf_op jit(solution)/shard_map/ppermute | solution.py:21
  195.0 120.6 %all-gather.11.cloned.1.call-start = ((), (), s32[]{:S(2)}) async-start(), calls=%async_computation.3 | async-start | bytes 2228224 | tf_op jit(solution)/shard_map/all_gather | solution.py:151
  210.3 105.3 %copy-start.25 = (s32[2048]{0:T(1024)S(1)}, s32[2048]{0:T(1024)}, u32[]{:S(2)}) copy-start(s32[2048]{0:T(1024)} %get-tuple-element.118) | copy-start | bytes 24580
  210.3 105.3 %copy-start.26 = (s32[2048]{0:T(1024)S(1)}, s32[2048]{0:T(1024)}, u32[]{:S(2)}) copy-start(s32[2048]{0:T(1024)} %fusion.85) | copy-start | bytes 24580
  210.3 105.3 %copy-start.27 = (s32[2048]{0:T(1024)S(1)}, s32[2048]{0:T(1024)}, u32[]{:S(2)}) copy-start(s32[2048]{0:T(1024)} %get-tuple-element.115) | copy-start | bytes 24580
  210.3 105.3 %copy-start.28 = (pred[2048]{0:T(1024)(128)(4,1)S(1)}, pred[2048]{0:T(1024)(128)(4,1)}, u32[]{:S(2)}) copy-start(pred[2048]{0:T(1024)(128)(4,1)} %get-tuple-element.135) | copy-start | bytes 6148
  210.3 105.3 %copy-start.31 = (s32[128]{0:T(128)S(1)}, s32[128]{0:T(128)}, u32[]{:S(2)}) copy-start(s32[128]{0:T(128)} %copy-done.30) | copy-start | bytes 1540
  210.3 105.3 %copy-start.32 = (s32[128]{0:T(128)S(1)}, s32[128]{0:T(128)}, u32[]{:S(2)}) copy-start(s32[128]{0:T(128)} %broadcast_in_dim.84) | copy-start | bytes 1540
  210.3 105.3 %copy-start.33 = (s32[128]{0:T(128)S(1)}, s32[128]{0:T(128)}, u32[]{:S(2)}) copy-start(s32[128]{0:T(128)} %broadcast.723) | copy-start | bytes 1540
  210.3 105.3 %copy-start.35 = (pred[128]{0:T(512)(128)(4,1)S(1)}, pred[128]{0:T(512)(128)(4,1)}, u32[]{:S(2)}) copy-start(pred[128]{0:T(512)(128)(4,1)} %copy-done.34) | copy-start | bytes 388
  323.4 7.0 %copy-start.3 = (f32[4,5,128,2048]{3,2,1,0:T(8,128)}, f32[4,5,128,2048]{3,2,1,0:T(8,128)S(1)}, u32[]{:S(2)}) copy-start(f32[4,5,128,2048]{3,2,1,0:T(8,128)S(1)} %get-tuple-element.122) | copy-start | bytes 62914564 | tf_op jit(solution)/shard_map/cond
  (17 other events, 31.9 us)
Sparse Core Ops, SparseCore 0:
  22.4 62.3 all-gather.4
  87.5 59.3 all-gather.6
  195.1 58.4 all-gather.8
  256.2 59.3 all-gather.10
where the time goes:
time: 361 us; the launch traced here: 358 us
  waiting for transfers between devices  177 us (49%)
  local copies, waits for them, and re-layouts  67.2 us (19%)
  matrix products  56.7 us (16%)
  other arithmetic  37.9 us (10%)
  between operations  17.1 us (5%)
    all_gather x2, waiting for transfers between devices, layer_call(): lax.all_gather(value_rows, 'seq', axis=0, tiled=True)  124 us
    all_gather x2, waiting for transfers between devices, layer_call(): lax.all_gather(key_rows, 'seq', axis=0, tiled=True)  50.1 us
    dot_general x4, matrix products, attend(): jnp.einsum('grnl,lgd->grnd', weights.astype(jnp.bfloat16), values_split,...  25.9 us
    unnamed x54, local copies, waits for them, and re-layouts  20.6 us
    dot_general x2, matrix products, project(): jnp.dot(normed, w_query, preferred_element_type=jnp.float32)  13.6 us
    reduce_sum x4, other arithmetic, attend(): total_new = total_now * rescale + jnp.sum(weights, axis=-1)  11.8 us
    reshape x4, local copies, waits for them, and re-layouts, attend(): values_split = value_rows.reshape(count, kv_heads, -1)  11.2 us
    dot_general x4, matrix products, attend(): jnp.einsum('grnd,lgd->grnl', query, keys_split, preferred_element_type=jn...  9.81 us
  transfers between devices with their start and end apart: 5, of which 5 were waited for; matrix products, arithmetic and copies ran while one was open for 19% of the time, Pallas kernels for 0%

commit v1 on v0

v1 whole, which is shorter than its diff:
```python
import functools

import jax
import jax.numpy as jnp
import numpy as np
from jax import lax
from jax.experimental import pallas as pl
from jax.experimental.pallas import tpu as pltpu
from jax.sharding import PartitionSpec as P

HS = 128
PB = 8
CB = 2
GROUP = 16
PLACES = PB + CB
PLANE = 4
PLANES = GROUP // PLANE

ROPE_BASE = 1000000.0
NEG = -1e30
EPS = 1e-06
MESH = pl.DeviceIdType.MESH
F32 = jnp.float32
BF16 = jnp.bfloat16


def rope_table(rows):
    half = HS // 2
    freqs = ROPE_BASE ** (-(np.arange(half) * 2.0 / HS))
    angles = np.arange(PLACES * rows)[:, None] * freqs[None, :]
    cosine, sine = np.cos(angles), np.sin(angles)
    table = np.stack([np.concatenate([cosine, cosine], 1), np.concatenate([-sine, sine], 1)])
    return table.reshape(2, PLACES, rows, HS).astype(np.float32)


def kernel(
    rows, kv_heads, repeat,
    owned, hidden, gain_ref, wq_hbm, wk_hbm, wv_hbm, table_ref,
    out_ref,
    x_s, normed, wq, wk, wv, q_s, keys, values, bias, top_s, total_s, acc_s,
    load_sem, send_sem, recv_sem, hand_sem,
):
    seg = lax.axis_index("segment")
    seq = lax.axis_index("seq")
    local = lax.rem(seq, GROUP)
    base = seq - local
    a, b, c = lax.rem(local, 2), lax.rem(local // 2, 2), local // PLANE
    head_cols = repeat * rows

    chunk = 4 * HS
    q_chunks = wq.shape[1] // chunk
    loads = [
        pltpu.make_async_copy(wk_hbm.at[0], wk, load_sem.at[1]),
        pltpu.make_async_copy(wv_hbm.at[0], wv, load_sem.at[2]),
    ] + [
        pltpu.make_async_copy(
            wq_hbm.at[0, :, pl.ds(i * chunk, chunk)], wq.at[:, pl.ds(i * chunk, chunk)], load_sem.at[3 + i]
        )
        for i in range(q_chunks)
    ]

    x_load = pltpu.make_async_copy(hidden, x_s, load_sem.at[0])

    @pl.when(seg == 0)
    def _():
        x_load.start()

    for load in loads:
        load.start()

    def device(a_of, b_of, c_of):
        return (seg, base + c_of * PLANE + b_of * 2 + a_of)

    x_dev, y_dev = device(1 - a, b, c), device(a, 1 - b, c)
    up_dev, down_dev = device(a, b, c + 1), device(a, b, c - 1)
    has_up, has_down = c < PLANES - 1, c > 0

    barrier = pltpu.get_barrier_semaphore()
    for target in (x_dev, y_dev, (1 - seg, seq)):
        pl.semaphore_signal(barrier, inc=1, device_id=target, device_id_type=MESH)

    @pl.when(has_up)
    def _():
        pl.semaphore_signal(barrier, inc=1, device_id=up_dev, device_id_type=MESH)

    @pl.when(has_down)
    def _():
        pl.semaphore_signal(barrier, inc=1, device_id=down_dev, device_id_type=MESH)

    pl.semaphore_wait(barrier, 3 + has_up.astype(jnp.int32) + has_down.astype(jnp.int32))

    buffers = (keys, values)

    def transfer(half, slot, target, direction, step, which):
        return pltpu.make_async_remote_copy(
            src_ref=buffers[half].at[slot],
            dst_ref=buffers[half].at[slot],
            send_sem=send_sem.at[direction, step, which],
            recv_sem=recv_sem.at[half, slot],
            device_id=target,
            device_id_type=MESH,
        )

    def arrived(half, slot):
        transfer(half, slot, x_dev, 0, 0, 0).wait_recv()

    def plane_at(step):
        if step == 0:
            return c
        low = {1: (1, 0), 2: (2, 2), 3: (3, 3)}[step]
        high = tuple(PLANES - 1 - p for p in low)
        return jnp.where(c == 0, low[0], jnp.where(c == 1, low[1], jnp.where(c == 2, high[1], high[0])))

    planes = [plane_at(step) for step in range(PLANES)]

    def slot_of(plane, a_of, b_of):
        return plane * PLANE + b_of * 2 + a_of

    def z_sends(half, step):
        plane = planes[step]
        slot = slot_of(plane, a, b)
        return (
            (has_up & (plane <= c), transfer(half, slot, up_dev, 2, step, half)),
            (has_down & (plane >= c), transfer(half, slot, down_dev, 3, step, half)),
        )

    def xy_sends(half, step):
        slot = slot_of(planes[step], a, b)
        return (transfer(half, slot, x_dev, 0, step, half), transfer(half, slot, y_dev, 1, step, half))

    def forwards(step):
        plane = planes[step]
        return (
            transfer(0, slot_of(plane, a, 1 - b), x_dev, 0, step, 2),
            transfer(1, slot_of(plane, 1 - a, b), y_dev, 1, step, 2),
        )

    def spread(half, step):
        if step > 0:
            arrived(half, slot_of(planes[step], a, b))
        for cond, copy in z_sends(half, step):
            pl.when(cond)(copy.start)
        for copy in xy_sends(half, step):
            copy.start()

    def relay(step):
        plane = planes[step]
        to_x, to_y = forwards(step)
        arrived(0, slot_of(plane, a, 1 - b))
        to_x.start()
        arrived(1, slot_of(plane, 1 - a, b))
        to_y.start()

    def gathered(step):
        plane = planes[step]
        arrived(0, slot_of(plane, 1 - a, b))
        arrived(1, slot_of(plane, a, 1 - b))
        arrived(0, slot_of(plane, 1 - a, 1 - b))
        arrived(1, slot_of(plane, 1 - a, 1 - b))

    hand = pltpu.make_async_remote_copy(
        src_ref=out_ref.at[0],
        dst_ref=x_s,
        send_sem=hand_sem.at[0],
        recv_sem=hand_sem.at[1],
        device_id=(1 - seg, seq),
        device_id_type=MESH,
    )

    mine = owned[seq]
    my_j = lax.rem(mine, GROUP)
    my_prompt = my_j < PB
    my_place = jnp.where(my_prompt, my_j, PB + lax.rem(my_j - PB + CB, CB))

    @pl.when(seg == 0)
    def _():
        x_load.wait()

    @pl.when(seg == 1)
    def _():
        hand.wait_recv()

    widened = x_s[...].astype(F32)
    meansq = jnp.mean(widened * widened, axis=-1, keepdims=True)
    normed[...] = (widened * lax.rsqrt(meansq + EPS) * gain_ref[...]).astype(BF16)

    cos_t = table_ref[0, my_place]
    sin_t = table_ref[1, my_place]

    def rotate(head):
        return head * cos_t + pltpu.roll(head, HS // 2, 1) * sin_t

    loads[0].wait()
    projected = jnp.dot(normed[...], wk[...], preferred_element_type=F32)
    for g in range(kv_heads):
        keys[local, :, g * HS : (g + 1) * HS] = rotate(projected[:, g * HS : (g + 1) * HS]).astype(BF16)
    spread(0, 0)
    loads[1].wait()
    values[local] = jnp.dot(normed[...], wv[...], preferred_element_type=F32).astype(BF16)
    spread(1, 0)

    def query_chunk(i):
        loads[2 + i].wait()
        projected = jnp.dot(normed[...], wq[:, i * chunk : (i + 1) * chunk], preferred_element_type=F32)
        for k in range(chunk // HS):
            q_s[i * (chunk // HS) + k] = (rotate(projected[:, k * HS : (k + 1) * HS]) * HS ** (-0.5)).astype(BF16)

    def attend(step):
        plane = planes[step]
        row = lax.broadcasted_iota(jnp.int32, (rows, rows), 0)
        col = lax.broadcasted_iota(jnp.int32, (rows, rows), 1)
        triangle = jnp.where(col <= row, 0.0, NEG).astype(F32)
        for i in range(PLANE):
            j = lax.rem(owned[base + plane * PLANE + i], GROUP)
            prompt = j < PB
            same = prompt == my_prompt
            pair = (j // CB) == (my_j // CB)
            full = jnp.where(prompt, (my_prompt == False) | (j < my_j), same & pair & (j < my_j))
            level = jnp.where(full, 0.0, NEG).astype(F32)
            bias[:, i * rows : (i + 1) * rows] = jnp.where(j == my_j, triangle, level)

        def one(g, carry):
            span = PLANE * rows
            cols = pl.ds(pl.multiple_of(g * HS, HS), HS)
            first = pl.multiple_of(plane * PLANE, PLANE)
            k_rows = keys[pl.ds(first, PLANE), :, cols].reshape(span, HS)
            v_rows = values[pl.ds(first, PLANE), :, cols].reshape(span, HS)
            query = q_s[pl.ds(g * repeat, repeat)].reshape(head_cols, HS)
            scores = lax.dot_general(query, k_rows, (((1,), (1,)), ((), ())), preferred_element_type=F32)
            scores = (scores.reshape(repeat, rows, span) + bias[...][None]).reshape(head_cols, span)
            best = jnp.max(scores, axis=-1, keepdims=True)
            if step == 0:
                top_new = jnp.broadcast_to(best, (head_cols, HS))
            else:
                top_old = top_s[g]
                top_new = jnp.maximum(top_old, best)
            weights = [jnp.exp(scores[:, i * HS : (i + 1) * HS] - top_new) for i in range(span // HS)]
            part = functools.reduce(jnp.add, weights)
            rounded = jnp.concatenate([w.astype(BF16) for w in weights], axis=1)
            update = jnp.dot(rounded, v_rows, preferred_element_type=F32)
            if step == 0:
                total_s[g] = part
                acc_s[g] = update
            else:
                rescale = jnp.exp(top_old - top_new)
                total_s[g] = total_s[g] * rescale + part
                acc_s[g] = acc_s[g] * rescale + update
            top_s[g] = top_new
            return carry

        lax.fori_loop(0, kv_heads, one, 0)

    half_way = (q_chunks + 1) // 2
    for i in range(half_way):
        query_chunk(i)
    relay(0)
    spread(0, 1)
    spread(1, 1)
    for i in range(half_way, q_chunks):
        query_chunk(i)
    for step in range(PLANES):
        gathered(step)
        attend(step)
        if step + 1 < PLANES:
            relay(step + 1)
            if step + 2 < PLANES:
                spread(0, step + 2)
                spread(1, step + 2)

    for g in range(kv_heads):
        total = jnp.sum(total_s[g], axis=-1, keepdims=True)
        mixed = acc_s[g] / total
        for r in range(repeat):
            lanes = slice((g * repeat + r) * HS, (g * repeat + r + 1) * HS)
            out_ref[0, :, lanes] = (
                x_s[:, lanes].astype(F32) + mixed[r * rows : (r + 1) * rows]
            ).astype(BF16)

    @pl.when(seg == 0)
    def _():
        hand.start()

    for step in range(PLANES):
        for half in range(2):
            for cond, copy in z_sends(half, step):
                pl.when(cond)(copy.wait_send)
            for copy in xy_sends(half, step):
                copy.wait_send()
        for copy in forwards(step):
            copy.wait_send()

    @pl.when(seg == 0)
    def _():
        hand.wait_send()


def section(hidden, norm_gain, query_weight, key_weight, value_weight, owned_block):
    rows, width = hidden.shape
    q_cols, kv_cols = query_weight.shape[2], key_weight.shape[2]
    heads, kv_heads = q_cols // HS, kv_cols // HS
    repeat = heads // kv_heads
    any_spec = pl.BlockSpec(memory_space=pl.ANY)
    vmem_spec = pl.BlockSpec(memory_space=pltpu.VMEM)
    state = pltpu.VMEM((kv_heads, repeat * rows, HS), F32)
    return pl.pallas_call(
        functools.partial(kernel, rows, kv_heads, repeat),
        out_shape=jax.ShapeDtypeStruct((1, rows, q_cols), BF16),
        in_specs=[
            pl.BlockSpec(memory_space=pltpu.SMEM),
            any_spec,
            vmem_spec,
            any_spec,
            any_spec,
            any_spec,
            vmem_spec,
        ],
        out_specs=vmem_spec,
        scratch_shapes=[
            pltpu.VMEM((rows, width), BF16),
            pltpu.VMEM((rows, width), BF16),
            pltpu.VMEM((width, q_cols), BF16),
            pltpu.VMEM((width, kv_cols), BF16),
            pltpu.VMEM((width, kv_cols), BF16),
            pltpu.VMEM((heads, rows, HS), BF16),
            pltpu.VMEM((GROUP, rows, kv_cols), BF16),
            pltpu.VMEM((GROUP, rows, kv_cols), BF16),
            pltpu.VMEM((rows, PLANE * rows), F32),
            state,
            state,
            state,
            pltpu.SemaphoreType.DMA((3 + q_cols // (4 * HS),)),
            pltpu.SemaphoreType.DMA((4, PLANES, 3)),
            pltpu.SemaphoreType.DMA((2, GROUP)),
            pltpu.SemaphoreType.DMA((2,)),
        ],
        compiler_params=pltpu.CompilerParams(
            collective_id=0, has_side_effects=True, vmem_limit_bytes=56 * 1024 * 1024
        ),
        cost_estimate=pl.CostEstimate(
            flops=2 * rows * width * (q_cols + 2 * kv_cols) + 4 * rows * rows * GROUP * q_cols,
            bytes_accessed=2 * width * (q_cols + 2 * kv_cols),
            transcendentals=rows * rows * GROUP * heads,
        ),
    )(owned_block, hidden, norm_gain, query_weight, key_weight, value_weight, jnp.asarray(rope_table(rows)))


def solution(mesh):
    return jax.shard_map(
        section,
        mesh=mesh,
        in_specs=(
            P("seq", None),
            P("segment", None),
            P("segment", None, None),
            P("segment", None, None),
            P("segment", None, None),
            P(),
        ),
        out_specs=P("segment", "seq", None),
        check_vma=False,
    )
```

time: 361 us -> 79.1 us (0.22)
  waiting for transfers between devices: 177 us -> 0 us
  Pallas kernels: 0 us -> 77 us
  local copies, waits for them, and re-layouts: 67.2 us -> 1.97 us
  matrix products: 56.7 us -> 0 us
  other arithmetic: 37.9 us -> 0 us
  between operations: 17.1 us -> 0.01 us
    all_gather x4 -> x0, waiting for transfers between devices: 174 us -> none  [the longest x2 124 us: layer_call(): lax.all_gather(value_rows, 'seq', axis=0, tiled=True)]
    pallas_call x0 -> x1, Pallas kernels: none -> 77 us  [section(): pl.pallas_call(functools.partial(kernel, rows, kv_heads, repeat), out_sha...]
    dot_general x14 -> x0, matrix products: 56.7 us -> none  [the longest x4 25.9 us: attend(): jnp.einsum('grnl,lgd->grnd', weights.astype(jnp.bfloat16), values_split,...]
    unnamed x54 -> x1, local copies, waits for them, and re-layouts: 20.6 us -> 1.97 us
    reshape x6 -> x0, local copies, waits for them, and re-layouts: 17.8 us -> none  [the longest x4 11.2 us: attend(): values_split = value_rows.reshape(count, kv_heads, -1)]
    reduce_sum x6 -> x0, other arithmetic: 12.5 us -> none  [the longest x4 11.8 us: attend(): total_new = total_now * rescale + jnp.sum(weights, axis=-1)]
    cond x22 -> x0, local copies, waits for them, and re-layouts: 8.6 us -> none  [the longest x2 4.57 us: fold_part(): return lax.cond(needed, take, leave, state_in)]
    concatenate x4 -> x0, local copies, waits for them, and re-layouts: 7.13 us -> none  [rotate(): jnp.concatenate([front * cosine - back * sine, back * cosine + front * si...]
  transfers between devices with their start and end apart: 5 -> 0, of which waited for: 5 -> 0; matrix products, arithmetic and copies ran while one was open for 19% -> 0% of each run, Pallas kernels for 0% -> 0%
where the time goes in v1:
time: 79.1 us; the launch traced here: 78.9 us
  Pallas kernels  77 us (97%)
  local copies, waits for them, and re-layouts  1.97 us (2%)
    pallas_call x1, Pallas kernels, section(): pl.pallas_call(functools.partial(kernel, rows, kv_heads, repeat), out_sha...  77 us
    unnamed x1, local copies, waits for them, and re-layouts  1.97 us

profile of v1, /device:TPU:1, one launch (start us, length us, event | category | flops | bytes accessed | tf_op | source)
XLA Modules:
  0.0 78.9 jit_solution(6118223120808111518)
XLA Ops:
  0.0 77.0 %shard_map.73 = bf16[1,128,2560]{2,1,0:T(8,128)(2,1)} custom-call(s32[16]{0:T(128)} %owned.1, bf16[128,2560]{1,0:T(8,128)(2,1)} %hidden.1, f32[1,2560]{1,0:T(1,128)} %gain_ref.1, bf16[1,2560,2560]{2,1,0:T(8,128)(2,1)} %wq_hbm.1, bf16[1,2560,512]{2,1,0:T(8,128)(2,1)} %wk_hbm.1, bf16[1,2560,512]{2,1,0:T(8,128)(2,1)} %wv_hbm.1, ...), custom_call_target="tpu_custom_call" | custom-call | flops 5033164800 | bytes 18350080 | tf_op jit(solution)/shard_map/pallas_call | solution.py:305
  77.0 2.0 %copy.9 = bf16[1,128,2560]{2,1,0:T(8,128)(2,1)} copy(bf16[1,128,2560]{2,1,0:T(8,128)(2,1)} %shard_map.73) | data formatting | bytes 1310720

commit v2 on v1

--- a/solution.py
+++ b/solution.py
@@ -18,7 +18,10 @@
 
 ROPE_BASE = 1000000.0
 NEG = -1e30
+SCALE = HS ** (-0.5) * float(np.log2(np.e))
 EPS = 1e-06
+UNROLL = 4
+REACH = 2
 MESH = pl.DeviceIdType.MESH
 F32 = jnp.float32
 BF16 = jnp.bfloat16
@@ -37,7 +40,7 @@
     rows, kv_heads, repeat,
     owned, hidden, gain_ref, wq_hbm, wk_hbm, wv_hbm, table_ref,
     out_ref,
-    x_s, normed, wq, wk, wv, q_s, keys, values, bias, top_s, total_s, acc_s,
+    x_s, normed, wq, wk, wv, q_s, keys, values, bias, top_s, acc_s,
     load_sem, send_sem, recv_sem, hand_sem,
 ):
     seg = lax.axis_index("segment")
@@ -135,6 +138,20 @@
             transfer(1, slot_of(plane, 1 - a, b), y_dev, 1, step, 2),
         )
 
+    def near(plane):
+        return (plane - c <= REACH) & (c - plane <= REACH)
+
+    def diagonals(step):
+        plane = planes[step]
+        slot = slot_of(plane, 1 - a, 1 - b)
+        go_up = has_up & (plane <= c) & (c + 1 - plane <= REACH)
+        go_down = has_down & (plane >= c) & (plane - c + 1 <= REACH)
+        return tuple(
+            (cond, transfer(half, slot, target, direction, step, 2 + half))
+            for half in range(2)
+            for cond, target, direction in ((go_up, up_dev, 2), (go_down, down_dev, 3))
+        )
+
     def spread(half, step):
         if step > 0:
             arrived(half, slot_of(planes[step], a, b))
@@ -147,9 +164,15 @@
         plane = planes[step]
         to_x, to_y = forwards(step)
         arrived(0, slot_of(plane, a, 1 - b))
-        to_x.start()
+        if step == 0:
+            to_x.start()
+        else:
+            pl.when(jnp.logical_not(near(plane)))(to_x.start)
         arrived(1, slot_of(plane, 1 - a, b))
-        to_y.start()
+        if step == 0:
+            to_y.start()
+        else:
+            pl.when(jnp.logical_not(near(plane)))(to_y.start)
 
     def gathered(step):
         plane = planes[step]
@@ -157,6 +180,9 @@
         arrived(1, slot_of(plane, a, 1 - b))
         arrived(0, slot_of(plane, 1 - a, 1 - b))
         arrived(1, slot_of(plane, 1 - a, 1 - b))
+        if step + 1 < PLANES:
+            for cond, copy in diagonals(step):
+                pl.when(cond)(copy.start)
 
     hand = pltpu.make_async_remote_copy(
         src_ref=out_ref.at[0],
@@ -199,17 +225,21 @@
     values[local] = jnp.dot(normed[...], wv[...], preferred_element_type=F32).astype(BF16)
     spread(1, 0)
 
+    eye = lax.broadcasted_iota(jnp.int32, (rows, rows), 0) == lax.broadcasted_iota(jnp.int32, (rows, rows), 1)
+    for h in range(kv_heads * repeat):
+        q_s[h, :, HS:] = eye.astype(F32).astype(BF16)
+
     def query_chunk(i):
         loads[2 + i].wait()
         projected = jnp.dot(normed[...], wq[:, i * chunk : (i + 1) * chunk], preferred_element_type=F32)
         for k in range(chunk // HS):
-            q_s[i * (chunk // HS) + k] = (rotate(projected[:, k * HS : (k + 1) * HS]) * HS ** (-0.5)).astype(BF16)
+            q_s[i * (chunk // HS) + k, :, :HS] = (rotate(projected[:, k * HS : (k + 1) * HS]) * SCALE).astype(BF16)
 
     def attend(step):
         plane = planes[step]
         row = lax.broadcasted_iota(jnp.int32, (rows, rows), 0)
         col = lax.broadcasted_iota(jnp.int32, (rows, rows), 1)
-        triangle = jnp.where(col <= row, 0.0, NEG).astype(F32)
+        triangle = jnp.where(row <= col, 0.0, NEG).astype(F32)
         for i in range(PLANE):
             j = lax.rem(owned[base + plane * PLANE + i], GROUP)
             prompt = j < PB
@@ -217,7 +247,7 @@
             pair = (j // CB) == (my_j // CB)
             full = jnp.where(prompt, (my_prompt == False) | (j < my_j), same & pair & (j < my_j))
             level = jnp.where(full, 0.0, NEG).astype(F32)
-            bias[:, i * rows : (i + 1) * rows] = jnp.where(j == my_j, triangle, level)
+            bias[i * rows : (i + 1) * rows] = jnp.where(j == my_j, triangle, level).astype(BF16)
 
         def one(g, carry):
             span = PLANE * rows
@@ -225,30 +255,28 @@
             first = pl.multiple_of(plane * PLANE, PLANE)
             k_rows = keys[pl.ds(first, PLANE), :, cols].reshape(span, HS)
             v_rows = values[pl.ds(first, PLANE), :, cols].reshape(span, HS)
-            query = q_s[pl.ds(g * repeat, repeat)].reshape(head_cols, HS)
-            scores = lax.dot_general(query, k_rows, (((1,), (1,)), ((), ())), preferred_element_type=F32)
-            scores = (scores.reshape(repeat, rows, span) + bias[...][None]).reshape(head_cols, span)
+            query = q_s[pl.ds(g * repeat, repeat)].reshape(head_cols, HS + rows)
+            k_wide = jnp.concatenate([k_rows, bias[...]], axis=1)
+            v_wide = jnp.concatenate([v_rows, jnp.ones((span, HS), BF16)], axis=1)
+            scores = lax.dot_general(query, k_wide, (((1,), (1,)), ((), ())), preferred_element_type=F32)
             best = jnp.max(scores, axis=-1, keepdims=True)
             if step == 0:
                 top_new = jnp.broadcast_to(best, (head_cols, HS))
             else:
                 top_old = top_s[g]
                 top_new = jnp.maximum(top_old, best)
-            weights = [jnp.exp(scores[:, i * HS : (i + 1) * HS] - top_new) for i in range(span // HS)]
-            part = functools.reduce(jnp.add, weights)
+            weights = [jnp.exp2(scores[:, i * HS : (i + 1) * HS] - top_new) for i in range(span // HS)]
             rounded = jnp.concatenate([w.astype(BF16) for w in weights], axis=1)
-            update = jnp.dot(rounded, v_rows, preferred_element_type=F32)
+            update = jnp.dot(rounded, v_wide, preferred_element_type=F32)
             if step == 0:
-                total_s[g] = part
                 acc_s[g] = update
             else:
-                rescale = jnp.exp(top_old - top_new)
-                total_s[g] = total_s[g] * rescale + part
-                acc_s[g] = acc_s[g] * rescale + update
+                rescale = jnp.exp2(top_old - top_new)
+                acc_s[g] = acc_s[g] * jnp.concatenate([rescale, rescale], axis=1) + update
             top_s[g] = top_new
             return carry
 
-        lax.fori_loop(0, kv_heads, one, 0)
+        lax.fori_loop(0, kv_heads, one, 0, unroll=UNROLL)
 
     half_way = (q_chunks + 1) // 2
     for i in range(half_way):
@@ -258,18 +286,24 @@
     spread(1, 1)
     for i in range(half_way, q_chunks):
         query_chunk(i)
-    for step in range(PLANES):
-        gathered(step)
-        attend(step)
-        if step + 1 < PLANES:
-            relay(step + 1)
-            if step + 2 < PLANES:
-                spread(0, step + 2)
-                spread(1, step + 2)
+    gathered(0)
+    spread(0, 2)
+    spread(1, 2)
+    spread(0, 3)
+    spread(1, 3)
+    attend(0)
+    relay(1)
+    gathered(1)
+    attend(1)
+    relay(2)
+    gathered(2)
+    relay(3)
+    attend(2)
+    gathered(3)
+    attend(3)
 
     for g in range(kv_heads):
-        total = jnp.sum(total_s[g], axis=-1, keepdims=True)
-        mixed = acc_s[g] / total
+        mixed = acc_s[g, :, :HS] / acc_s[g, :, HS:]
         for r in range(repeat):
             lanes = slice((g * repeat + r) * HS, (g * repeat + r + 1) * HS)
             out_ref[0, :, lanes] = (
@@ -286,8 +320,14 @@
                 pl.when(cond)(copy.wait_send)
             for copy in xy_sends(half, step):
                 copy.wait_send()
+        if step + 1 < PLANES:
+            for cond, copy in diagonals(step):
+                pl.when(cond)(copy.wait_send)
         for copy in forwards(step):
-            copy.wait_send()
+            if step == 0:
+                copy.wait_send()
+            else:
+                pl.when(jnp.logical_not(near(planes[step])))(copy.wait_send)
 
     @pl.when(seg == 0)
     def _():
@@ -301,7 +341,6 @@
     repeat = heads // kv_heads
     any_spec = pl.BlockSpec(memory_space=pl.ANY)
     vmem_spec = pl.BlockSpec(memory_space=pltpu.VMEM)
-    state = pltpu.VMEM((kv_heads, repeat * rows, HS), F32)
     return pl.pallas_call(
         functools.partial(kernel, rows, kv_heads, repeat),
         out_shape=jax.ShapeDtypeStruct((1, rows, q_cols), BF16),
@@ -321,15 +360,14 @@
             pltpu.VMEM((width, q_cols), BF16),
             pltpu.VMEM((width, kv_cols), BF16),
             pltpu.VMEM((width, kv_cols), BF16),
-            pltpu.VMEM((heads, rows, HS), BF16),
+            pltpu.VMEM((heads, rows, HS + rows), BF16),
             pltpu.VMEM((GROUP, rows, kv_cols), BF16),
             pltpu.VMEM((GROUP, rows, kv_cols), BF16),
-            pltpu.VMEM((rows, PLANE * rows), F32),
-            state,
-            state,
-            state,
+            pltpu.VMEM((PLANE * rows, rows), BF16),
+            pltpu.VMEM((kv_heads, repeat * rows, HS), F32),
+            pltpu.VMEM((kv_heads, repeat * rows, 2 * HS), F32),
             pltpu.SemaphoreType.DMA((3 + q_cols // (4 * HS),)),
-            pltpu.SemaphoreType.DMA((4, PLANES, 3)),
+            pltpu.SemaphoreType.DMA((4, PLANES, 4)),
             pltpu.SemaphoreType.DMA((2, GROUP)),
             pltpu.SemaphoreType.DMA((2,)),
         ],

time: 79.1 us -> 69.3 us (0.88)
  Pallas kernels: 77 us -> 67.1 us
    pallas_call x1, Pallas kernels: 77 us -> 67.1 us  [section(): pl.pallas_call(functools.partial(kernel, rows, kv_heads, repeat), out_sha...]
where the time goes in v2:
time: 69.3 us; the launch traced here: 69.1 us
  Pallas kernels  67.1 us (97%)
  local copies, waits for them, and re-layouts  1.97 us (3%)
    pallas_call x1, Pallas kernels, section(): pl.pallas_call(functools.partial(kernel, rows, kv_heads, repeat), out_sha...  67.1 us
    unnamed x1, local copies, waits for them, and re-layouts  1.97 us

profile of v2, /device:TPU:1, one launch (start us, length us, event | category | flops | bytes accessed | tf_op | source)
XLA Modules:
  0.0 69.1 jit_solution(10770449136320875842)
XLA Ops:
  0.0 67.1 %shard_map.73 = bf16[1,128,2560]{2,1,0:T(8,128)(2,1)} custom-call(s32[16]{0:T(128)} %owned.1, bf16[128,2560]{1,0:T(8,128)(2,1)} %hidden.1, f32[1,2560]{1,0:T(1,128)} %gain_ref.1, bf16[1,2560,2560]{2,1,0:T(8,128)(2,1)} %wq_hbm.1, bf16[1,2560,512]{2,1,0:T(8,128)(2,1)} %wk_hbm.1, bf16[1,2560,512]{2,1,0:T(8,128)(2,1)} %wv_hbm.1, ...), custom_call_target="tpu_custom_call" | custom-call | flops 5033164800 | bytes 18350080 | tf_op jit(solution)/shard_map/pallas_call | solution.py:344
  67.2 2.0 %copy.9 = bf16[1,128,2560]{2,1,0:T(8,128)(2,1)} copy(bf16[1,128,2560]{2,1,0:T(8,128)(2,1)} %shard_map.73) | data formatting | bytes 1310720

commit v3 on v2

--- a/solution.py
+++ b/solution.py
@@ -68,7 +68,7 @@
     def _():
         x_load.start()
 
-    for load in loads:
+    for load in loads[:2]:
         load.start()
 
     def device(a_of, b_of, c_of):
@@ -217,6 +217,8 @@
         return head * cos_t + pltpu.roll(head, HS // 2, 1) * sin_t
 
     loads[0].wait()
+    for load in loads[2:]:
+        load.start()
     projected = jnp.dot(normed[...], wk[...], preferred_element_type=F32)
     for g in range(kv_heads):
         keys[local, :, g * HS : (g + 1) * HS] = rotate(projected[:, g * HS : (g + 1) * HS]).astype(BF16)
@@ -235,13 +237,12 @@
         for k in range(chunk // HS):
             q_s[i * (chunk // HS) + k, :, :HS] = (rotate(projected[:, k * HS : (k + 1) * HS]) * SCALE).astype(BF16)
 
-    def attend(step):
-        plane = planes[step]
+    def attend(step, first, count):
         row = lax.broadcasted_iota(jnp.int32, (rows, rows), 0)
         col = lax.broadcasted_iota(jnp.int32, (rows, rows), 1)
         triangle = jnp.where(row <= col, 0.0, NEG).astype(F32)
-        for i in range(PLANE):
-            j = lax.rem(owned[base + plane * PLANE + i], GROUP)
+        for i in range(count):
+            j = lax.rem(owned[base + first + i], GROUP)
             prompt = j < PB
             same = prompt == my_prompt
             pair = (j // CB) == (my_j // CB)
@@ -250,13 +251,12 @@
             bias[i * rows : (i + 1) * rows] = jnp.where(j == my_j, triangle, level).astype(BF16)
 
         def one(g, carry):
-            span = PLANE * rows
+            span = count * rows
             cols = pl.ds(pl.multiple_of(g * HS, HS), HS)
-            first = pl.multiple_of(plane * PLANE, PLANE)
-            k_rows = keys[pl.ds(first, PLANE), :, cols].reshape(span, HS)
-            v_rows = values[pl.ds(first, PLANE), :, cols].reshape(span, HS)
+            k_rows = keys[pl.ds(first, count), :, cols].reshape(span, HS)
+            v_rows = values[pl.ds(first, count), :, cols].reshape(span, HS)
             query = q_s[pl.ds(g * repeat, repeat)].reshape(head_cols, HS + rows)
-            k_wide = jnp.concatenate([k_rows, bias[...]], axis=1)
+            k_wide = jnp.concatenate([k_rows, bias[:span]], axis=1)
             v_wide = jnp.concatenate([v_rows, jnp.ones((span, HS), BF16)], axis=1)
             scores = lax.dot_general(query, k_wide, (((1,), (1,)), ((), ())), preferred_element_type=F32)
             best = jnp.max(scores, axis=-1, keepdims=True)
@@ -291,16 +291,21 @@
     spread(1, 2)
     spread(0, 3)
     spread(1, 3)
-    attend(0)
+    attend(0, planes[0] * PLANE, PLANE)
     relay(1)
     gathered(1)
-    attend(1)
+    attend(1, planes[1] * PLANE, PLANE)
     relay(2)
     gathered(2)
     relay(3)
-    attend(2)
-    gathered(3)
-    attend(3)
+    attend(2, planes[2] * PLANE, PLANE)
+    last = planes[3] * PLANE
+    arrived(0, slot_of(planes[3], 1 - a, b))
+    attend(3, last + 2 * b, 2)
+    arrived(1, slot_of(planes[3], a, 1 - b))
+    arrived(0, slot_of(planes[3], 1 - a, 1 - b))
+    arrived(1, slot_of(planes[3], 1 - a, 1 - b))
+    attend(3, last + 2 * (1 - b), 2)
 
     for g in range(kv_heads):
         mixed = acc_s[g, :, :HS] / acc_s[g, :, HS:]

time: 69.3 us -> 67.2 us (0.970)
  Pallas kernels: 67.1 us -> 65 us
    pallas_call x1, Pallas kernels: 67.1 us -> 65 us  [section(): pl.pallas_call(functools.partial(kernel, rows, kv_heads, repeat), out_sha...]
where the time goes in v3:
time: 67.2 us; the launch traced here: 67 us
  Pallas kernels  65 us (97%)
  local copies, waits for them, and re-layouts  1.97 us (3%)
    pallas_call x1, Pallas kernels, section(): pl.pallas_call(functools.partial(kernel, rows, kv_heads, repeat), out_sha...  65 us
    unnamed x1, local copies, waits for them, and re-layouts  1.97 us

profile of v3, /device:TPU:1, one launch (start us, length us, event | category | flops | bytes accessed | tf_op | source)
XLA Modules:
  0.0 67.0 jit_solution(7526269979518319702)
XLA Ops:
  0.0 65.0 %shard_map.73 = bf16[1,128,2560]{2,1,0:T(8,128)(2,1)} custom-call(s32[16]{0:T(128)} %owned.1, bf16[128,2560]{1,0:T(8,128)(2,1)} %hidden.1, f32[1,2560]{1,0:T(1,128)} %gain_ref.1, bf16[1,2560,2560]{2,1,0:T(8,128)(2,1)} %wq_hbm.1, bf16[1,2560,512]{2,1,0:T(8,128)(2,1)} %wk_hbm.1, bf16[1,2560,512]{2,1,0:T(8,128)(2,1)} %wv_hbm.1, ...), custom_call_target="tpu_custom_call" | custom-call | flops 5033164800 | bytes 18350080 | tf_op jit(solution)/shard_map/pallas_call | solution.py:349
  65.0 2.0 %copy.9 = bf16[1,128,2560]{2,1,0:T(8,128)(2,1)} copy(bf16[1,128,2560]{2,1,0:T(8,128)(2,1)} %shard_map.73) | data formatting | bytes 1310720
